TPU v7x, 32 devices: a whole 2x2x4 slice. The times are simulated.
32 devices in a mesh: dp: 4 (over y, core), wide: 4 (over z), narrow: 2 (over x).
Axes of the slice: x: 2, y: 2, z: 4, core: 2. Of those that a mesh axis runs over, the one named last changes fastest.
Arguments:
- streams: bfloat16 [4, 1024, 2048], P(None, 'dp', ('wide', 'narrow')), may hold values from -6 to 6
- prior: bfloat16 [12, 1024, 2048], P(None, 'dp', ('wide', 'narrow')), may hold values from -6 to 6
- streams_grad: bfloat16 [4, 1024, 2048], P(None, 'dp', ('wide', 'narrow')), may hold values from -6 to 6
- w_qkv: bfloat16 [3, 2048, 2048], P(None, 'wide', 'narrow')
- qkv_bias: bfloat16 [3, 2048], P(None, ('narrow', 'wide')), may hold values from -3 to 3
- w_out: bfloat16 [2048, 2048], P('narrow', 'wide'), may hold values from -1.5 to 1.5
- w_up: bfloat16 [2048, 8192], P('wide', 'narrow')
- up_bias: bfloat16 [8192], P(('narrow', 'wide')), may hold values from -3 to 3
- w_down: bfloat16 [8192, 2048], P('narrow', 'wide'), may hold values from -0.0625 to 0.0625
- branch_bias: bfloat16 [2048], P(('wide', 'narrow')), may hold values from -3 to 3
- norm_gain: bfloat16 [4, 2048], P(None, ('wide', 'narrow')), may hold values from 0.25 to 1.75
- norm_bias: bfloat16 [4, 2048], P(None, ('wide', 'narrow')), may hold values from -2 to 2
- mix_gain: bfloat16 [2048], P(('wide', 'narrow')), may hold values from 0.099609375 to 1.8984375
- mix_in: bfloat16 [2048, 52], P(('wide', 'narrow')), may hold values from -0.125 to 0.125
- mix_out: bfloat16 [52, 52], replicated, may hold values from -0.875 to 0.875
- mix_static: bfloat16 [52], replicated, may hold values from -3 to 3
Outputs:
- streams_out: bfloat16 [4, 1024, 2048], P(None, 'dp', ('wide', 'narrow'))
- streams_in_grad: bfloat16 [4, 1024, 2048], P(None, 'dp', ('wide', 'narrow'))
- prior_grad: bfloat16 [12, 1024, 2048], P(None, 'dp', ('wide', 'narrow'))
- w_qkv_grad: float32 [3, 2048, 2048], P(None, 'wide', 'narrow')
- qkv_bias_grad: float32 [3, 2048], P(None, ('narrow', 'wide'))
- w_out_grad: float32 [2048, 2048], P('narrow', 'wide')
- w_up_grad: float32 [2048, 8192], P('wide', 'narrow')
- up_bias_grad: float32 [8192], P(('narrow', 'wide'))
- w_down_grad: float32 [8192, 2048], P('narrow', 'wide')
- branch_bias_grad: float32 [2048], P(('wide', 'narrow'))
- norm_gain_grad: float32 [4, 2048], P(None, ('wide', 'narrow'))
- norm_bias_grad: float32 [4, 2048], P(None, ('wide', 'narrow'))
- mix_gain_grad: float32 [2048], P(('wide', 'narrow'))
- mix_in_grad: float32 [2048, 52], P(('wide', 'narrow'))
- mix_out_grad: float32 [52, 52], replicated
- mix_static_grad: float32 [52], replicated
All inputs are finite; a program needn't handle non-finite values.
Results may differ from a plain program's by a relative error of at most 0.02.
Values may be sent and summed in bfloat16 or wider, within the bound.
No kernel may reach another device: no remote copies, remote signals or barrier semaphores. Data moves between devices by JAX's collectives and lax.ppermute only.
A program may use at most 192 MiB of HBM per device.

v0:
```python
import math
import jax
import jax.numpy as jnp
from jax import lax
from jax.sharding import PartitionSpec as P

D = 2048
HD = 128
ROT = 32
MIXH = 52
STACK = 13
norm_eps = 1e-05
rms_eps = 1e-06


def model_sum(parts):
    return lax.psum(parts, ("wide", "narrow"))


def gelu_exact(inputs):
    return 0.5 * inputs * (1.0 + lax.erf(inputs * (1.0 / math.sqrt(2.0))))


def gelu_slope(inputs):
    normal_cdf = 0.5 * (1.0 + lax.erf(inputs * (1.0 / math.sqrt(2.0))))
    return normal_cdf + inputs * jnp.exp(-0.5 * inputs * inputs) * (1.0 / math.sqrt(2.0 * math.pi))


def rotate(heads_in, cosine, sine_table, direction):
    half = ROT // 2
    first = heads_in[..., :half]
    second = heads_in[..., half:ROT]
    rest_part = heads_in[..., ROT:]
    cos_b = cosine[:, None, :]
    sin_b = direction * sine_table[:, None, :]
    return jnp.concatenate(
        [first * cos_b - second * sin_b, second * cos_b + first * sin_b, rest_part], axis=-1
    )


def masked_scores(query_rows, key_heads, row_start, row_block, length, scale):
    scores = (
        jnp.einsum("qhd,khd->hqk", query_rows, key_heads, preferred_element_type=jnp.float32)
        * scale
    )
    row_ids = row_start + lax.broadcasted_iota(jnp.int32, (row_block, length), 0)
    col_ids = lax.broadcasted_iota(jnp.int32, (row_block, length), 1)
    return jnp.where((col_ids <= row_ids)[None], scores, -1e30)


def attend_rows(queries, key_heads, value_heads, scale):
    length = queries.shape[0]
    row_block = min(512, length)

    def one_block(block_index):
        row_start = block_index * row_block
        scores = masked_scores(queries, key_heads, row_start, row_block, length, scale)
        row_top = jnp.max(scores, axis=2, keepdims=True)
        log_total = row_top + jnp.log(jnp.sum(jnp.exp(scores - row_top), axis=2, keepdims=True))
        attn_probs = jnp.exp(scores - log_total).astype(jnp.bfloat16)
        output = jnp.einsum(
            "hqk,khd->qhd", attn_probs, value_heads, preferred_element_type=jnp.float32
        )
        return (output, log_total[:, :, 0])

    outputs, totals = lax.map(one_block, jnp.arange(length // row_block, dtype=jnp.int32))
    return (outputs.reshape(queries.shape), totals)


def attend_back(queries, key_heads, value_heads, out_grad, totals, scale):
    length = queries.shape[0]
    row_block = min(512, length)

    def one_block(carry, block_index):
        key_grad, value_grad = carry
        row_start = block_index * row_block
        log_total = lax.dynamic_index_in_dim(totals, block_index, 0, keepdims=False)
        scores = masked_scores(queries, key_heads, row_start, row_block, length, scale)
        attn_probs = jnp.exp(scores - log_total[:, :, None])
        probs_low = attn_probs.astype(jnp.bfloat16)
        value_grad = value_grad + jnp.einsum(
            "hqk,qhd->khd", probs_low, out_grad, preferred_element_type=jnp.float32
        )
        prob_grad = jnp.einsum(
            "qhd,khd->hqk", out_grad, value_heads, preferred_element_type=jnp.float32
        )
        row_dot = jnp.sum(attn_probs * prob_grad, axis=2, keepdims=True)
        score_grad = (attn_probs * (prob_grad - row_dot)).astype(jnp.bfloat16)
        query_grad = (
            jnp.einsum("hqk,khd->qhd", score_grad, key_heads, preferred_element_type=jnp.float32)
            * scale
        )
        key_grad = (
            key_grad
            + jnp.einsum("hqk,qhd->khd", score_grad, queries, preferred_element_type=jnp.float32)
            * scale
        )
        return ((key_grad, value_grad), query_grad)

    zero_heads = jnp.zeros(queries.shape, jnp.float32)
    (key_grad, value_grad), query_blocks = lax.scan(
        one_block, (zero_heads, zero_heads), jnp.arange(length // row_block, dtype=jnp.int32)
    )
    return (query_blocks.reshape(queries.shape), key_grad, value_grad)


def contract_rows(left, right):
    return lax.dot_general(
        left, right, (((0,), (0,)), ((), ())), preferred_element_type=jnp.float32
    )


def contract_cols(left, right):
    return lax.dot_general(
        left, right, (((1,), (1,)), ((), ())), preferred_element_type=jnp.float32
    )


def per_device(
    streams,
    prior,
    streams_grad,
    w_qkv,
    qkv_bias,
    w_out,
    w_up,
    up_bias,
    w_down,
    branch_bias,
    norm_gain,
    norm_bias,
    mix_gain,
    mix_in,
    mix_out,
    mix_static,
):
    high = lax.Precision.HIGHEST
    length = streams.shape[1]
    local_cols = streams.shape[2]
    heads_here = local_cols // HD
    scale = 1.0 / math.sqrt(HD)
    inputs = streams.astype(jnp.float32)
    row_total, row_squares = model_sum((jnp.sum(inputs, axis=2), jnp.sum(inputs * inputs, axis=2)))
    row_mean = row_total / D
    inv_std = lax.rsqrt(row_squares / D - row_mean * row_mean + norm_eps)
    centred = (inputs - row_mean[:, :, None]) * inv_std[:, :, None]
    norm_scale = norm_gain.astype(jnp.float32)[:, None, :]
    normed = (centred * norm_scale + norm_bias.astype(jnp.float32)[:, None, :]).astype(jnp.bfloat16)
    near_cols = lax.all_gather(normed, "narrow", axis=2, tiled=True)
    qkv_part = jnp.einsum("std,sdf->stf", near_cols[:3], w_qkv, preferred_element_type=jnp.float32)
    up_part = jnp.dot(near_cols[3], w_up, preferred_element_type=jnp.float32)
    qkv_pre, up_summed = (
        lax.psum_scatter(qkv_part, "wide", scatter_dimension=2, tiled=True),
        lax.psum_scatter(up_part[None], "wide", scatter_dimension=2, tiled=True),
    )
    up_pre = up_summed[0]
    qkv_pre = qkv_pre + qkv_bias.astype(jnp.float32)[:, None, :]
    up_pre = up_pre + up_bias.astype(jnp.float32)[None, :]
    positions = lax.iota(jnp.float32, length)
    freqs = jnp.exp(lax.iota(jnp.float32, ROT // 2) * (-2.0 * math.log(10000.0) / ROT))
    angles = positions[:, None] * freqs[None, :]
    cosine = jnp.cos(angles)
    sine_table = jnp.sin(angles)
    head_view = qkv_pre.reshape(3, length, heads_here, HD)
    queries = rotate(head_view[0], cosine, sine_table, 1.0).astype(jnp.bfloat16)
    key_heads = rotate(head_view[1], cosine, sine_table, 1.0).astype(jnp.bfloat16)
    value_heads = head_view[2].astype(jnp.bfloat16)
    attn_heads, totals = attend_rows(queries, key_heads, value_heads, scale)
    attn_low = attn_heads.reshape(length, local_cols).astype(jnp.bfloat16)
    hidden = gelu_exact(up_pre).astype(jnp.bfloat16)
    attn_wide, hidden_wide = (
        lax.all_gather(attn_low, "wide", axis=1, tiled=True),
        lax.all_gather(hidden, "wide", axis=1, tiled=True),
    )
    branch_part = jnp.dot(attn_wide, w_out, preferred_element_type=jnp.float32) + jnp.dot(
        hidden_wide, w_down, preferred_element_type=jnp.float32
    )
    branch = (
        lax.psum_scatter(branch_part, "narrow", scatter_dimension=1, tiled=True)
        + branch_bias.astype(jnp.float32)[None, :]
    )
    layer_out = inputs[3] + branch
    mix_scale = mix_gain.astype(jnp.float32)
    scaled = layer_out * mix_scale[None, :]
    mix_weight = mix_in.astype(jnp.float32)
    mix_back = mix_out.astype(jnp.float32)
    energy, logit_sum = model_sum(
        (jnp.sum(layer_out * layer_out, axis=1), jnp.dot(scaled, mix_weight, precision=high))
    )
    rms = lax.rsqrt(energy / D + rms_eps)
    logits = logit_sum * rms[:, None]
    mix_hidden = gelu_exact(logits)
    weights = (
        jnp.dot(mix_hidden, mix_back, precision=high) + mix_static.astype(jnp.float32)[None, :]
    )
    coef = weights.reshape(length, 4, STACK)
    prior_vals = prior.astype(jnp.float32)
    mixed = jnp.einsum("tsj,jtl->stl", coef[:, :, : STACK - 1], prior_vals, precision=high)
    streams_out = (
        mixed + jnp.transpose(coef[:, :, STACK - 1])[:, :, None] * layer_out[None]
    ).astype(jnp.bfloat16)
    grad_out = streams_grad.astype(jnp.float32)
    prior_part = jnp.einsum("stl,jtl->tsj", grad_out, prior_vals, precision=high)
    layer_part = jnp.einsum("stl,tl->ts", grad_out, layer_out, precision=high)
    coef_part = jnp.concatenate([prior_part, layer_part[:, :, None]], axis=2).reshape(length, MIXH)
    (coef_grad,) = model_sum((coef_part,))
    prior_grad = jnp.einsum(
        "tsj,stl->jtl", coef[:, :, : STACK - 1], grad_out, precision=high
    ).astype(jnp.bfloat16)
    layer_grad = jnp.einsum("ts,stl->tl", coef[:, :, STACK - 1], grad_out, precision=high)
    static_grad = jnp.sum(coef_grad, axis=0)
    mix_out_grad = jnp.dot(mix_hidden.T, coef_grad, precision=high)
    logit_grad = jnp.dot(coef_grad, mix_back.T, precision=high) * gelu_slope(logits)
    sum_grad = logit_grad * rms[:, None]
    rms_grad = jnp.sum(logit_grad * logit_sum, axis=1)
    energy_grad = -0.5 * rms_grad * rms * rms * rms / D
    mix_in_grad = jnp.dot(scaled.T, sum_grad, precision=high)
    scaled_grad = jnp.dot(sum_grad, mix_weight.T, precision=high)
    mix_gain_grad = jnp.sum(scaled_grad * layer_out, axis=0)
    layer_grad = (
        layer_grad + scaled_grad * mix_scale[None, :] + 2.0 * energy_grad[:, None] * layer_out
    )
    branch_grad = layer_grad.astype(jnp.bfloat16)
    branch_bias_grad = jnp.sum(branch_grad.astype(jnp.float32), axis=0)
    branch_near = lax.all_gather(branch_grad, "narrow", axis=1, tiled=True)
    attn_grad, hidden_grad = (
        lax.psum_scatter(
            contract_cols(branch_near, w_out), "wide", scatter_dimension=1, tiled=True
        ),
        lax.psum_scatter(
            contract_cols(branch_near, w_down), "wide", scatter_dimension=1, tiled=True
        ),
    )
    out_weight_grad = contract_rows(attn_wide, branch_near)
    down_weight_grad = contract_rows(hidden_wide, branch_near)
    attn_low_grad = attn_grad.astype(jnp.bfloat16).reshape(length, heads_here, HD)
    up_grad = (hidden_grad * gelu_slope(up_pre)).astype(jnp.bfloat16)
    up_bias_grad = jnp.sum(up_grad.astype(jnp.float32), axis=0)
    query_grad, key_grad, value_grad = attend_back(
        queries, key_heads, value_heads, attn_low_grad, totals, scale
    )
    query_pre = rotate(query_grad, cosine, sine_table, -1.0).reshape(length, local_cols)
    key_pre = rotate(key_grad, cosine, sine_table, -1.0).reshape(length, local_cols)
    projected_grad = jnp.stack([query_pre, key_pre, value_grad.reshape(length, local_cols)]).astype(
        jnp.bfloat16
    )
    qkv_bias_grad = jnp.sum(projected_grad.astype(jnp.float32), axis=1)
    far_qkv, far_up = (
        lax.all_gather(projected_grad, "wide", axis=2, tiled=True),
        lax.all_gather(up_grad[None], "wide", axis=2, tiled=True),
    )
    qkv_weight_grad = jnp.einsum(
        "std,stf->sdf", near_cols[:3], far_qkv, preferred_element_type=jnp.float32
    )
    up_weight_grad = contract_rows(near_cols[3], far_up[0])
    normed_part = jnp.concatenate(
        [
            jnp.einsum("stf,sdf->std", far_qkv, w_qkv, preferred_element_type=jnp.float32),
            contract_cols(far_up[0], w_up)[None],
        ],
        axis=0,
    )
    normed_grad = lax.psum_scatter(normed_part, "narrow", scatter_dimension=2, tiled=True)
    gain_grad = jnp.sum(normed_grad * centred, axis=1)
    shift_grad = jnp.sum(normed_grad, axis=1)
    centred_grad = normed_grad * norm_scale
    grad_total, grad_cross = model_sum(
        (jnp.sum(centred_grad, axis=2), jnp.sum(centred_grad * centred, axis=2))
    )
    input_grad = inv_std[:, :, None] * (
        centred_grad - (grad_total / D)[:, :, None] - centred * (grad_cross / D)[:, :, None]
    )
    input_grad = input_grad.at[3].add(layer_grad)
    streams_in_grad = input_grad.astype(jnp.bfloat16)
    summed = lax.psum(
        (
            qkv_weight_grad,
            qkv_bias_grad,
            out_weight_grad,
            up_weight_grad,
            up_bias_grad,
            down_weight_grad,
            branch_bias_grad,
            gain_grad,
            shift_grad,
            mix_gain_grad,
            mix_in_grad,
            mix_out_grad,
            static_grad,
        ),
        "dp",
    )
    return (
        streams_out,
        streams_in_grad,
        prior_grad,
        summed[0],
        summed[1],
        summed[2],
        summed[3],
        summed[4],
        summed[5],
        summed[6],
        summed[7],
        summed[8],
        summed[9],
        summed[10],
        summed[11],
        summed[12],
    )


def solution(mesh):
    return jax.shard_map(
        per_device,
        mesh=mesh,
        in_specs=(
            P(None, "dp", ("wide", "narrow")),
            P(None, "dp", ("wide", "narrow")),
            P(None, "dp", ("wide", "narrow")),
            P(None, "wide", "narrow"),
            P(None, ("narrow", "wide")),
            P("narrow", "wide"),
            P("wide", "narrow"),
            P(("narrow", "wide")),
            P("narrow", "wide"),
            P(("wide", "narrow")),
            P(None, ("wide", "narrow")),
            P(None, ("wide", "narrow")),
            P(("wide", "narrow")),
            P(("wide", "narrow"), None),
            P(),
            P(),
        ),
        out_specs=(
            P(None, "dp", ("wide", "narrow")),
            P(None, "dp", ("wide", "narrow")),
            P(None, "dp", ("wide", "narrow")),
            P(None, "wide", "narrow"),
            P(None, ("narrow", "wide")),
            P("narrow", "wide"),
            P("wide", "narrow"),
            P(("narrow", "wide")),
            P("narrow", "wide"),
            P(("wide", "narrow")),
            P(None, ("wide", "narrow")),
            P(None, ("wide", "narrow")),
            P(("wide", "narrow")),
            P(("wide", "narrow"), None),
            P(),
            P(),
        ),
        check_vma=False,
    )
```

profile of v0, /device:TPU:0, one launch (start us, length us, event | category | flops | bytes accessed | tf_op | source)
XLA Modules:
  0.0 1101.8 jit_solution(11456983785825005663)
XLA Ops:
  10.2 23.3 %all-reduce.2 = (f32[4,256]{1,0:T(4,128)S(1)}, f32[4,256]{1,0:T(4,128)S(1)}) all-reduce(f32[4,256]{1,0:T(4,128)S(1)} %get-tuple-element.142, f32[4,256]{1,0:T(4,128)S(1)} %get-tuple-element.141), channel_id=1, replica_groups=mesh['dp'=4,'wide'=4,'narrow'=2] {'wide','narrow'}, use_global_device_ids=true, to_apply=%region_3.0 | all-reduce | flops 2048 | bytes 16384 | tf_op jit(solution)/shard_map/psum | solution.py:17
  35.8 18.7 %all-gather.6.cloned.1.call-done = bf16[4,256,512]{2,1,0:T(8,128)(2,1)} async-done(((bf16[4,256,256]{2,1,0:T(8,128)(2,1)}), bf16[4,256,512]{2,1,0:T(8,128)(2,1)}) %all-gather.6.cloned.1.call-update) | async-done | bytes 1048592 | tf_op jit(solution)/shard_map/all_gather | solution.py:149
  54.4 5.6 convolution_bitcast_fusion
  64.6 72.4 %reduce-scatter.9.cloned.1.call-done = f32[1,256,1024]{2,1,0:T(8,128)} async-done(((f32[1,256,4096]{2,1,0:T(8,128)}), f32[1,256,1024]{2,1,0:T(8,128)}) %reduce-scatter.9.cloned.1.call-update) | async-done | bytes 1048592 | tf_op jit(solution)/shard_map/reduce_scatter | solution.py:154
  141.1 59.6 %reduce-scatter.7.cloned.1.call-done = f32[3,256,256]{2,1,0:T(8,128)} async-done(((f32[3,256,1024]{2,1,0:T(8,128)}), f32[3,256,256]{2,1,0:T(8,128)}) %reduce-scatter.7.cloned.1.call-update) | async-done | bytes 786448 | tf_op jit(solution)/shard_map/reduce_scatter | solution.py:153
  214.0 22.1 %all_gather.19 = bf16[256,1024]{0,1:T(8,128)(2,1)} all-gather(bf16[256,256]{0,1:T(8,128)(2,1)S(1)} %bitcast.112), channel_id=1, replica_groups=mesh['dp'=4,'wide'=4,'narrow'=2] {'wide'}, dimensions={1}, use_global_device_ids=true | all-gather | bytes 655360 | tf_op jit(solution)/shard_map/all_gather | solution.py:172
  236.2 20.9 %all-gather.8.cloned.1.call-done = bf16[256,4096]{1,0:T(8,128)(2,1)} async-done(((bf16[256,1024]{1,0:T(8,128)(2,1)}), bf16[256,4096]{1,0:T(8,128)(2,1)}) %all-gather.8.cloned.1.call-update) | async-done | bytes 2097168 | tf_op jit(solution)/shard_map/all_gather | solution.py:173
  257.1 4.2 fusion.66
  269.6 6.5 reduce-scatter.11.cloned.1.call-done
  288.1 68.3 %all-reduce.9.cloned.1.call-done = (f32[256,52]{0,1:T(8,128)}, f32[256]{0:T(256)}, f32[256,52]{0,1:T(8,128)}) async-done(((f32[256,52]{0,1:T(8,128)}, f32[256]{0:T(256)}, f32[256,52]{0,1:T(8,128)}), (f32[256,52]{0,1:T(8,128)}, f32[256]{0:T(256)}, f32[256,52]{0,1:T(8,128)})) %all-reduce.9.cloned.1.call-update) | async-done | bytes 107536 | tf_op jit(solution)/shard_map/psum | solution.py:17
  370.7 5.6 all_gather.21
  377.9 5.5 fusion.69
  383.4 21.7 %reduce-scatter.13.cloned.1.call-done = f32[256,256]{1,0:T(8,128)} async-done(((f32[256,1024]{1,0:T(8,128)}), f32[256,256]{1,0:T(8,128)}) %reduce-scatter.13.cloned.1.call-update) | async-done | bytes 262160 | tf_op jit(solution)/shard_map/reduce_scatter | solution.py:227
  425.3 58.1 %reduce-scatter.15.cloned.1.call-done = f32[256,1024]{1,0:T(8,128)} async-done(((f32[256,4096]{1,0:T(8,128)}), f32[256,1024]{1,0:T(8,128)}) %reduce-scatter.15.cloned.1.call-update) | async-done | bytes 1048592 | tf_op jit(solution)/shard_map/reduce_scatter | solution.py:230
  487.0 36.9 %all-gather.10.cloned.1.call-done = bf16[3,256,1024]{2,1,0:T(8,128)(2,1)} async-done(((bf16[3,256,256]{2,1,0:T(8,128)(2,1)}), bf16[3,256,1024]{2,1,0:T(8,128)(2,1)}) %all-gather.10.cloned.1.call-update) | async-done | bytes 1572880 | tf_op jit(solution)/shard_map/all_gather | solution.py:249
  527.5 42.7 %all-gather.12.cloned.1.call-done = bf16[256,4096]{1,0:T(8,128)(2,1)} async-done(((bf16[256,1024]{1,0:T(8,128)(2,1)}), bf16[256,4096]{1,0:T(8,128)(2,1)}) %all-gather.12.cloned.1.call-update) | async-done | bytes 2097168 | tf_op jit(solution)/shard_map/all_gather | solution.py:250
  570.2 4.1 convolution_bitcast_fusion.1
  580.9 4.7 fusion.71
  589.4 17.2 %reduce-scatter.17.cloned.1.call-done = f32[4,256,256]{2,1,0:T(8,128)} async-done(((f32[4,256,512]{2,1,0:T(8,128)}), f32[4,256,256]{2,1,0:T(8,128)}) %reduce-scatter.17.cloned.1.call-update) | async-done | bytes 1048592 | tf_op jit(solution)/shard_map/reduce_scatter | solution.py:263
  609.3 5.6 fusion.31
  626.4 20.7 %all-reduce = (f32[4,256]{1,0:T(4,128)S(1)}, f32[4,256]{1,0:T(4,128)S(1)}) all-reduce(f32[4,256]{1,0:T(4,128)S(1)} %get-tuple-element.138, f32[4,256]{1,0:T(4,128)S(1)} %get-tuple-element.139), channel_id=1, replica_groups=mesh['dp'=4,'wide'=4,'narrow'=2] {'wide','narrow'}, use_global_device_ids=true, to_apply=%region_21.22 | all-reduce | flops 2048 | bytes 16384 | tf_op jit(solution)/shard_map/psum | solution.py:17
  648.8 423.5 %all-reduce.13.cloned.1.call-done = (f32[3,512,1024]{2,1,0:T(8,128)}, f32[1024,512]{1,0:T(8,128)}, f32[512,4096]{1,0:T(8,128)}, f32[4096,512]{1,0:T(8,128)}) async-done(((f32[3,512,1024]{2,1,0:T(8,128)}, f32[1024,512]{1,0:T(8,128)}, f32[512,4096]{1,0:T(8,128)}, f32[4096,512]{1,0:T(8,128)}), (f32[3,512,1024]{2,1,0:T(8,128)}, f32[1024,512]{1,0:T(8,128)}, f32[512,4096]{1,0:T(8,128)}, ...) | async-done | bytes 25165840 | tf_op jit(solution)/shard_map/psum | solution.py:275
  1072.3 7.1 copy.244
  1081.3 4.3 copy.247
  (248 shorter events, 128.0 us)
Async XLA Ops:
  7.2 52.9 %copy-start = (bf16[3,512,1024]{2,1,0:T(8,128)(2,1)S(1)}, bf16[3,512,1024]{2,1,0:T(8,128)(2,1)}, u32[]{:S(2)}) copy-start(bf16[3,512,1024]{2,1,0:T(8,128)(2,1)} %param.21) | copy-start | bytes 9437188
  7.2 47.2 %all-gather.6.cloned.1.call-start = ((), (), s32[]{:S(2)}) async-start(), calls=%async_computation.6 | async-start | bytes 1572864 | tf_op jit(solution)/shard_map/all_gather | solution.py:149
  35.7 101.2 %reduce-scatter.9.cloned.1.call-start = ((), (), s32[]{:S(2)}) async-start(), calls=%async_computation.8 | async-start | bytes 5242880 | tf_op jit(solution)/shard_map/reduce_scatter | solution.py:154
  60.0 140.7 %reduce-scatter.7.cloned.1.call-start = ((), (), s32[]{:S(2)}) async-start(), calls=%async_computation.7 | async-start | bytes 3932160 | tf_op jit(solution)/shard_map/reduce_scatter | solution.py:153
  63.9 75.4 %copy-start.52 = (bf16[3,256]{1,0:T(4,128)(2,1)S(1)}, bf16[3,256]{1,0:T(4,128)(2,1)}, u32[]{:S(2)}) copy-start(bf16[3,256]{1,0:T(4,128)(2,1)} %param.22) | copy-start | bytes 4612
  63.9 193.2 %all-gather.8.cloned.1.call-start = ((), (), s32[]{:S(2)}) async-start(), calls=%async_computation.9 | async-start | bytes 2621440 | tf_op jit(solution)/shard_map/all_gather | solution.py:173
  64.6 138.0 %copy-start.41 = (f32[1024]{0:T(1024)}, f32[1024]{0:T(1024)S(1)}, u32[]{:S(2)}) copy-start(f32[1024]{0:T(1024)S(1)} %convert_element_type.100) | copy-start | bytes 12292
  139.2 136.9 %reduce-scatter.11.cloned.1.call-start = ((), (), s32[]{:S(2)}) async-start(), calls=%async_computation.10 | async-start | bytes 786432 | tf_op jit(solution)/shard_map/reduce_scatter | solution.py:179
  262.6 93.8 %all-reduce.9.cloned.1.call-start = ((), (), s32[]{:S(2)}) async-start(), calls=%async_computation.16 | async-start | bytes 231424 | tf_op jit(solution)/shard_map/psum | solution.py:17
  277.9 90.4 %copy-start.9 = (f32[256,256]{1,0:T(8,128)}, f32[256,256]{1,0:T(8,128)S(1)}, u32[]{:S(2)}) copy-start(f32[256,256]{1,0:T(8,128)S(1)} %get-tuple-element.171) | copy-start | bytes 786436
  286.7 118.5 %reduce-scatter.13.cloned.1.call-start = ((), (), s32[]{:S(2)}) async-start(), calls=%async_computation.11 | async-start | bytes 1310720 | tf_op jit(solution)/shard_map/reduce_scatter | solution.py:227
  365.9 10.5 copy-start.12
  377.8 105.6 %reduce-scatter.15.cloned.1.call-start = ((), (), s32[]{:S(2)}) async-start(), calls=%async_computation.13 | async-start | bytes 5242880 | tf_op jit(solution)/shard_map/reduce_scatter | solution.py:230
  383.4 140.5 %all-gather.10.cloned.1.call-start = ((), (), s32[]{:S(2)}) async-start(), calls=%async_computation.12 | async-start | bytes 1966080 | tf_op jit(solution)/shard_map/all_gather | solution.py:249
  425.3 144.9 %all-gather.12.cloned.1.call-start = ((), (), s32[]{:S(2)}) async-start(), calls=%async_computation.15 | async-start | bytes 2621440 | tf_op jit(solution)/shard_map/all_gather | solution.py:250
  486.9 119.6 %reduce-scatter.17.cloned.1.call-start = ((), (), s32[]{:S(2)}) async-start(), calls=%async_computation.14 | async-start | bytes 3145728 | tf_op jit(solution)/shard_map/reduce_scatter | solution.py:263
  527.5 46.8 %copy-start.5 = (f32[3,256,512]{2,1,0:T(8,128)S(1)}, f32[3,256,512]{2,1,0:T(8,128)}, u32[]{:S(2)}) copy-start(f32[3,256,512]{2,1,0:T(8,128)} %fusion.68) | copy-start | bytes 4718596
  575.9 72.9 %all-reduce.11.cloned.1.call-start = ((), (), s32[]{:S(2)}) async-start(), calls=%async_computation.17 | async-start | bytes 209920 | tf_op jit(solution)/shard_map/psum | solution.py:275
  585.6 21.0 %copy-start.3 = (bf16[4,256,256]{2,1,0:T(8,128)(2,1)S(1)}, bf16[4,256,256]{2,1,0:T(8,128)(2,1)}, u32[]{:S(2)}) copy-start(bf16[4,256,256]{2,1,0:T(8,128)(2,1)} %param.18) | copy-start | bytes 1572868
  585.6 23.7 %copy-start.15 = (bf16[256,4096]{1,0:T(8,128)(2,1)S(1)}, bf16[256,4096]{1,0:T(8,128)(2,1)}, u32[]{:S(2)}) copy-start(bf16[256,4096]{1,0:T(8,128)(2,1)} %all-gather.12.cloned.1.call-done) | copy-start | bytes 6291460
  609.2 463.0 %all-reduce.13.cloned.1.call-start = ((), (), s32[]{:S(2)}) async-start(), calls=%async_computation.18 | async-start | bytes 50331648 | tf_op jit(solution)/shard_map/psum | solution.py:275
  621.9 25.3 %copy-start.8 = (f32[4,256,256]{2,1,0:T(8,128)S(1)}, f32[4,256,256]{2,1,0:T(8,128)}, u32[]{:S(2)}) copy-start(f32[4,256,256]{2,1,0:T(8,128)} %reduce-scatter.17.cloned.1.call-done) | copy-start | bytes 3145732
  625.5 22.3 %copy-start.30 = (f32[256,256]{1,0:T(8,128)S(1)}, f32[256,256]{1,0:T(8,128)}, u32[]{:S(2)}) copy-start(f32[256,256]{1,0:T(8,128)} %get-tuple-element.165) | copy-start | bytes 786436
  1072.3 9.0 copy-start.4
  (49 other events, 169.3 us)
Sparse Core Ops, SparseCore 0:
  35.8 18.5 all-gather.5
  60.1 76.7 reduce-scatter.8
  139.9 60.7 reduce-scatter.6
  202.8 54.2 all-gather.7
  262.7 13.3 reduce-scatter.10
  286.8 69.5 all-reduce.8
  377.9 27.1 reduce-scatter.12
  408.0 75.4 reduce-scatter.14
  485.7 38.1 all-gather.9
  526.0 44.1 all-gather.11
  576.0 30.5 reduce-scatter.16
  610.6 30.8 all-reduce.10
  645.6 426.6 all-reduce.12
where the time goes:
time: 1100 us
  waiting for transfers between devices  847 us (77%)
  matrix products  75 us (7%)
  blocking collectives  71.8 us (7%)
  local copies, waits for them, and re-layouts  54.5 us (5%)
  other arithmetic  38.3 us (3%)
  between operations  14.6 us (1%)
    psum x2, waiting for transfers between devices, per_device(): lax.psum((qkv_weight_grad, qkv_bias_grad, out_weight_grad, up_weight_grad...  423 us
    reduce_scatter x1, waiting for transfers between devices, per_device(): lax.psum_scatter(up_part[None], 'wide', scatter_dimension=2, tiled=True)  72.4 us
    psum x1, waiting for transfers between devices, model_sum(): return lax.psum(parts, ('wide', 'narrow'))  68.3 us
    reduce_scatter x1, waiting for transfers between devices, per_device(): lax.psum_scatter(qkv_part, 'wide', scatter_dimension=2, tiled=True)  59.6 us
    reduce_scatter x1, waiting for transfers between devices, per_device(): lax.psum_scatter(contract_cols(branch_near, w_down), 'wide', scatter_dime...  58.1 us
    psum x2, blocking collectives, model_sum(): return lax.psum(parts, ('wide', 'narrow'))  44 us
    all_gather x1, waiting for transfers between devices, per_device(): lax.all_gather(up_grad[None], 'wide', axis=2, tiled=True)  42.7 us
    all_gather x1, waiting for transfers between devices, per_device(): lax.all_gather(projected_grad, 'wide', axis=2, tiled=True)  36.9 us
  transfers between devices with their start and end apart: 13, of which 12 were waited for; matrix products, arithmetic and copies ran while one was open for 8% of the time, Pallas kernels for 0%

commit v1 on v0

--- a/solution.py
+++ b/solution.py
@@ -14,7 +14,7 @@
 
 
 def model_sum(parts):
-    return lax.psum(parts, ("wide", "narrow"))
+    return lax.psum(lax.psum(parts, "narrow"), "wide")
 
 
 def gelu_exact(inputs):

time: 1100 us -> 1090 us (level)
    psum x1 -> x2, waiting for transfers between devices: 68.3 us -> 57.4 us  [model_sum(): return lax.psum(lax.psum(parts, 'narrow'), 'wide')]
    psum x2 -> x4, blocking collectives: 44 us -> 35.3 us  [model_sum(): return lax.psum(lax.psum(parts, 'narrow'), 'wide')]
  transfers between devices with their start and end apart: 13 -> 14, of which waited for: 12 -> 13; matrix products, arithmetic and copies ran while one was open for 8% -> 8% of each run, Pallas kernels for 0% -> 0%
where the time goes in v1:
time: 1090 us
  waiting for transfers between devices  841 us (77%)
  matrix products  75 us (7%)
  blocking collectives  63.1 us (6%)
  local copies, waits for them, and re-layouts  54.5 us (5%)
  other arithmetic  38.3 us (4%)
  between operations  14.6 us (1%)
    psum x2, waiting for transfers between devices, per_device(): lax.psum((qkv_weight_grad, qkv_bias_grad, out_weight_grad, up_weight_grad...  427 us
    reduce_scatter x1, waiting for transfers between devices, per_device(): lax.psum_scatter(up_part[None], 'wide', scatter_dimension=2, tiled=True)  72.4 us
    reduce_scatter x1, waiting for transfers between devices, per_device(): lax.psum_scatter(qkv_part, 'wide', scatter_dimension=2, tiled=True)  59.6 us
    reduce_scatter x1, waiting for transfers between devices, per_device(): lax.psum_scatter(contract_cols(branch_near, w_down), 'wide', scatter_dime...  58.2 us
    psum x2, waiting for transfers between devices, model_sum(): return lax.psum(lax.psum(parts, 'narrow'), 'wide')  57.4 us
    all_gather x1, waiting for transfers between devices, per_device(): lax.all_gather(up_grad[None], 'wide', axis=2, tiled=True)  42.9 us
    all_gather x1, waiting for transfers between devices, per_device(): lax.all_gather(projected_grad, 'wide', axis=2, tiled=True)  36.8 us
    psum x4, blocking collectives, model_sum(): return lax.psum(lax.psum(parts, 'narrow'), 'wide')  35.3 us
  transfers between devices with their start and end apart: 14, of which 13 were waited for; matrix products, arithmetic and copies ran while one was open for 8% of the time, Pallas kernels for 0%

profile of v1, /device:TPU:0, one launch (start us, length us, event | category | flops | bytes accessed | tf_op | source)
XLA Modules:
  0.0 1087.2 jit_solution(10209145720767926508)
XLA Ops:
  10.2 5.9 all-reduce.7
  16.0 12.6 %all-reduce.2 = (f32[4,256]{1,0:T(4,128)S(1)}, f32[4,256]{1,0:T(4,128)S(1)}) all-reduce(f32[4,256]{1,0:T(4,128)S(1)} %get-tuple-element.168, f32[4,256]{1,0:T(4,128)S(1)} %get-tuple-element.169), channel_id=1, replica_groups=mesh['dp'=4,'wide'=4,'narrow'=2] {'wide'}, use_global_device_ids=true, to_apply=%region_5.0 | all-reduce | flops 2048 | bytes 16384 | tf_op jit(solution)/shard_map/psum | solution.py:17
  31.0 19.6 %all-gather.6.cloned.1.call-done = bf16[4,256,512]{2,1,0:T(8,128)(2,1)} async-done(((bf16[4,256,256]{2,1,0:T(8,128)(2,1)}), bf16[4,256,512]{2,1,0:T(8,128)(2,1)}) %all-gather.6.cloned.1.call-update) | async-done | bytes 1048592 | tf_op jit(solution)/shard_map/all_gather | solution.py:149
  50.6 5.6 convolution_bitcast_fusion
  60.7 72.4 %reduce-scatter.9.cloned.1.call-done = f32[1,256,1024]{2,1,0:T(8,128)} async-done(((f32[1,256,4096]{2,1,0:T(8,128)}), f32[1,256,1024]{2,1,0:T(8,128)}) %reduce-scatter.9.cloned.1.call-update) | async-done | bytes 1048592 | tf_op jit(solution)/shard_map/reduce_scatter | solution.py:154
  137.2 59.6 %reduce-scatter.7.cloned.1.call-done = f32[3,256,256]{2,1,0:T(8,128)} async-done(((f32[3,256,1024]{2,1,0:T(8,128)}), f32[3,256,256]{2,1,0:T(8,128)}) %reduce-scatter.7.cloned.1.call-update) | async-done | bytes 786448 | tf_op jit(solution)/shard_map/reduce_scatter | solution.py:153
  210.2 22.1 %all_gather.19 = bf16[256,1024]{0,1:T(8,128)(2,1)} all-gather(bf16[256,256]{0,1:T(8,128)(2,1)S(1)} %bitcast.112), channel_id=1, replica_groups=mesh['dp'=4,'wide'=4,'narrow'=2] {'wide'}, dimensions={1}, use_global_device_ids=true | all-gather | bytes 655360 | tf_op jit(solution)/shard_map/all_gather | solution.py:172
  232.3 20.9 %all-gather.8.cloned.1.call-done = bf16[256,4096]{1,0:T(8,128)(2,1)} async-done(((bf16[256,1024]{1,0:T(8,128)(2,1)}), bf16[256,4096]{1,0:T(8,128)(2,1)}) %all-gather.8.cloned.1.call-update) | async-done | bytes 2097168 | tf_op jit(solution)/shard_map/all_gather | solution.py:173
  265.7 6.5 reduce-scatter.11.cloned.1.call-done
  282.8 21.6 %all-reduce.19.cloned.1.call-done = (f32[256,52]{0,1:T(8,128)}, f32[256]{0:T(256)}, f32[256,52]{0,1:T(8,128)}) async-done(((f32[256,52]{0,1:T(8,128)}, f32[256]{0:T(256)}, f32[256,52]{0,1:T(8,128)}), (f32[256,52]{0,1:T(8,128)}, f32[256]{0:T(256)}, f32[256,52]{0,1:T(8,128)})) %all-reduce.19.cloned.1.call-update) | async-done | bytes 107536 | tf_op jit(solution)/shard_map/psum | solution.py:17
  305.9 35.8 %all-reduce.13.cloned.1.call-done = (f32[256,52]{0,1:T(8,128)}, f32[256]{0:T(256)}, f32[256,52]{0,1:T(8,128)}) async-done(((f32[256,52]{0,1:T(8,128)}, f32[256]{0:T(256)}, f32[256,52]{0,1:T(8,128)}), (f32[256,52]{0,1:T(8,128)}, f32[256]{0:T(256)}, f32[256,52]{0,1:T(8,128)})) %all-reduce.13.cloned.1.call-update) | async-done | bytes 107536 | tf_op jit(solution)/shard_map/psum | solution.py:17
  355.9 5.6 all_gather.21
  363.1 5.5 fusion.69
  368.6 21.8 %reduce-scatter.13.cloned.1.call-done = f32[256,256]{1,0:T(8,128)} async-done(((f32[256,1024]{1,0:T(8,128)}), f32[256,256]{1,0:T(8,128)}) %reduce-scatter.13.cloned.1.call-update) | async-done | bytes 262160 | tf_op jit(solution)/shard_map/reduce_scatter | solution.py:227
  410.6 58.2 %reduce-scatter.15.cloned.1.call-done = f32[256,1024]{1,0:T(8,128)} async-done(((f32[256,4096]{1,0:T(8,128)}), f32[256,1024]{1,0:T(8,128)}) %reduce-scatter.15.cloned.1.call-update) | async-done | bytes 1048592 | tf_op jit(solution)/shard_map/reduce_scatter | solution.py:230
  472.3 36.8 %all-gather.10.cloned.1.call-done = bf16[3,256,1024]{2,1,0:T(8,128)(2,1)} async-done(((bf16[3,256,256]{2,1,0:T(8,128)(2,1)}), bf16[3,256,1024]{2,1,0:T(8,128)(2,1)}) %all-gather.10.cloned.1.call-update) | async-done | bytes 1572880 | tf_op jit(solution)/shard_map/all_gather | solution.py:249
  512.7 42.9 %all-gather.12.cloned.1.call-done = bf16[256,4096]{1,0:T(8,128)(2,1)} async-done(((bf16[256,1024]{1,0:T(8,128)(2,1)}), bf16[256,4096]{1,0:T(8,128)(2,1)}) %all-gather.12.cloned.1.call-update) | async-done | bytes 2097168 | tf_op jit(solution)/shard_map/all_gather | solution.py:250
  566.2 4.7 fusion.71
  574.7 17.2 %reduce-scatter.17.cloned.1.call-done = f32[4,256,256]{2,1,0:T(8,128)} async-done(((f32[4,256,512]{2,1,0:T(8,128)}), f32[4,256,256]{2,1,0:T(8,128)}) %reduce-scatter.17.cloned.1.call-update) | async-done | bytes 1048592 | tf_op jit(solution)/shard_map/reduce_scatter | solution.py:263
  594.6 5.6 fusion.31
  611.8 5.0 all-reduce.5
  616.7 11.8 %all-reduce = (f32[4,256]{1,0:T(4,128)S(1)}, f32[4,256]{1,0:T(4,128)S(1)}) all-reduce(f32[4,256]{1,0:T(4,128)S(1)} %get-tuple-element.163, f32[4,256]{1,0:T(4,128)S(1)} %get-tuple-element.164), channel_id=1, replica_groups=mesh['dp'=4,'wide'=4,'narrow'=2] {'wide'}, use_global_device_ids=true, to_apply=%region_28.29 | all-reduce | flops 2048 | bytes 16384 | tf_op jit(solution)/shard_map/psum | solution.py:17
  630.3 427.4 %all-reduce.17.cloned.1.call-done = (f32[3,512,1024]{2,1,0:T(8,128)}, f32[1024,512]{1,0:T(8,128)}, f32[512,4096]{1,0:T(8,128)}, f32[4096,512]{1,0:T(8,128)}) async-done(((f32[3,512,1024]{2,1,0:T(8,128)}, f32[1024,512]{1,0:T(8,128)}, f32[512,4096]{1,0:T(8,128)}, f32[4096,512]{1,0:T(8,128)}), (f32[3,512,1024]{2,1,0:T(8,128)}, f32[1024,512]{1,0:T(8,128)}, f32[512,4096]{1,0:T(8,128)}, ...) | async-done | bytes 25165840 | tf_op jit(solution)/shard_map/psum | solution.py:275
  1057.6 7.1 copy.247
  (253 shorter events, 140.5 us)
Async XLA Ops:
  7.2 49.0 %copy-start = (bf16[3,512,1024]{2,1,0:T(8,128)(2,1)S(1)}, bf16[3,512,1024]{2,1,0:T(8,128)(2,1)}, u32[]{:S(2)}) copy-start(bf16[3,512,1024]{2,1,0:T(8,128)(2,1)} %param.21) | copy-start | bytes 9437188
  7.2 43.4 %all-gather.6.cloned.1.call-start = ((), (), s32[]{:S(2)}) async-start(), calls=%async_computation.6 | async-start | bytes 1572864 | tf_op jit(solution)/shard_map/all_gather | solution.py:149
  30.9 102.1 %reduce-scatter.9.cloned.1.call-start = ((), (), s32[]{:S(2)}) async-start(), calls=%async_computation.8 | async-start | bytes 5242880 | tf_op jit(solution)/shard_map/reduce_scatter | solution.py:154
  56.1 140.7 %reduce-scatter.7.cloned.1.call-start = ((), (), s32[]{:S(2)}) async-start(), calls=%async_computation.7 | async-start | bytes 3932160 | tf_op jit(solution)/shard_map/reduce_scatter | solution.py:153
  60.0 75.4 %copy-start.52 = (bf16[3,256]{1,0:T(4,128)(2,1)S(1)}, bf16[3,256]{1,0:T(4,128)(2,1)}, u32[]{:S(2)}) copy-start(bf16[3,256]{1,0:T(4,128)(2,1)} %param.22) | copy-start | bytes 4612
  60.0 193.2 %all-gather.8.cloned.1.call-start = ((), (), s32[]{:S(2)}) async-start(), calls=%async_computation.9 | async-start | bytes 2621440 | tf_op jit(solution)/shard_map/all_gather | solution.py:173
  60.7 138.0 %copy-start.41 = (f32[1024]{0:T(1024)}, f32[1024]{0:T(1024)S(1)}, u32[]{:S(2)}) copy-start(f32[1024]{0:T(1024)S(1)} %convert_element_type.100) | copy-start | bytes 12292
  135.3 136.9 %reduce-scatter.11.cloned.1.call-start = ((), (), s32[]{:S(2)}) async-start(), calls=%async_computation.10 | async-start | bytes 786432 | tf_op jit(solution)/shard_map/reduce_scatter | solution.py:179
  258.7 45.7 %all-reduce.19.cloned.1.call-start = ((), (), s32[]{:S(2)}) async-start(), calls=%async_computation.19 | async-start | bytes 231424 | tf_op jit(solution)/shard_map/psum | solution.py:17
  274.0 79.5 %copy-start.9 = (f32[256,256]{1,0:T(8,128)}, f32[256,256]{1,0:T(8,128)S(1)}, u32[]{:S(2)}) copy-start(f32[256,256]{1,0:T(8,128)S(1)} %get-tuple-element.178) | copy-start | bytes 786436
  282.8 58.9 %all-reduce.13.cloned.1.call-start = ((), (), s32[]{:S(2)}) async-start(), calls=%async_computation.16 | async-start | bytes 231424 | tf_op jit(solution)/shard_map/psum | solution.py:17
  304.5 86.0 %reduce-scatter.13.cloned.1.call-start = ((), (), s32[]{:S(2)}) async-start(), calls=%async_computation.11 | async-start | bytes 1310720 | tf_op jit(solution)/shard_map/reduce_scatter | solution.py:227
  351.1 10.5 copy-start.12
  363.0 105.8 %reduce-scatter.15.cloned.1.call-start = ((), (), s32[]{:S(2)}) async-start(), calls=%async_computation.13 | async-start | bytes 5242880 | tf_op jit(solution)/shard_map/reduce_scatter | solution.py:230
  368.6 140.5 %all-gather.10.cloned.1.call-start = ((), (), s32[]{:S(2)}) async-start(), calls=%async_computation.12 | async-start | bytes 1966080 | tf_op jit(solution)/shard_map/all_gather | solution.py:249
  410.6 145.0 %all-gather.12.cloned.1.call-start = ((), (), s32[]{:S(2)}) async-start(), calls=%async_computation.15 | async-start | bytes 2621440 | tf_op jit(solution)/shard_map/all_gather | solution.py:250
  472.3 119.7 %reduce-scatter.17.cloned.1.call-start = ((), (), s32[]{:S(2)}) async-start(), calls=%async_computation.14 | async-start | bytes 3145728 | tf_op jit(solution)/shard_map/reduce_scatter | solution.py:263
  512.7 47.0 %copy-start.5 = (f32[3,256,512]{2,1,0:T(8,128)S(1)}, f32[3,256,512]{2,1,0:T(8,128)}, u32[]{:S(2)}) copy-start(f32[3,256,512]{2,1,0:T(8,128)} %fusion.68) | copy-start | bytes 4718596
  561.2 69.0 %all-reduce.15.cloned.1.call-start = ((), (), s32[]{:S(2)}) async-start(), calls=%async_computation.17 | async-start | bytes 209920 | tf_op jit(solution)/shard_map/psum | solution.py:275
  570.9 21.0 %copy-start.3 = (bf16[4,256,256]{2,1,0:T(8,128)(2,1)S(1)}, bf16[4,256,256]{2,1,0:T(8,128)(2,1)}, u32[]{:S(2)}) copy-start(bf16[4,256,256]{2,1,0:T(8,128)(2,1)} %param.18) | copy-start | bytes 1572868
  570.9 23.7 %copy-start.15 = (bf16[256,4096]{1,0:T(8,128)(2,1)S(1)}, bf16[256,4096]{1,0:T(8,128)(2,1)}, u32[]{:S(2)}) copy-start(bf16[256,4096]{1,0:T(8,128)(2,1)} %all-gather.12.cloned.1.call-done) | copy-start | bytes 6291460
  594.6 463.1 %all-reduce.17.cloned.1.call-start = ((), (), s32[]{:S(2)}) async-start(), calls=%async_computation.18 | async-start | bytes 50331648 | tf_op jit(solution)/shard_map/psum | solution.py:275
  607.2 21.4 %copy-start.8 = (f32[4,256,256]{2,1,0:T(8,128)S(1)}, f32[4,256,256]{2,1,0:T(8,128)}, u32[]{:S(2)}) copy-start(f32[4,256,256]{2,1,0:T(8,128)} %reduce-scatter.17.cloned.1.call-done) | copy-start | bytes 3145732
  610.9 18.4 %copy-start.30 = (f32[256,256]{1,0:T(8,128)S(1)}, f32[256,256]{1,0:T(8,128)}, u32[]{:S(2)}) copy-start(f32[256,256]{1,0:T(8,128)} %get-tuple-element.172) | copy-start | bytes 786436
  (50 other events, 178.2 us)
Sparse Core Ops, SparseCore 0:
  31.0 19.4 all-gather.5
  56.3 76.7 reduce-scatter.8
  136.1 60.7 reduce-scatter.6
  198.9 54.2 all-gather.7
  258.8 13.3 reduce-scatter.10
  282.9 21.4 all-reduce.18
  307.0 34.6 all-reduce.12
  363.1 27.2 reduce-scatter.12
  393.3 75.4 reduce-scatter.14
  470.9 38.1 all-gather.9
  511.3 44.1 all-gather.11
  561.3 30.5 reduce-scatter.16
  596.1 30.8 all-reduce.14
  631.0 426.6 all-reduce.16
